TPU v7x, 512 devices: a whole 4x4x16 slice. The times are simulated.
512 devices in a mesh: ctx: 64 (over z_hi, x, y, core), head: 8 (over z_lo).
Axes of the slice: x: 4, y: 4, z: 16 (z_hi: 2, z_lo: 8; z = z_hi * 8 + z_lo), core: 2. Of those that a mesh axis runs over, the one named last changes fastest.
Arguments:
- query_rows: bfloat16 [32768, 4096], P('ctx', 'head'), may hold values from -32 to 32
- key_rows: bfloat16 [32768, 1024], P('ctx', 'head'), may hold values from -32 to 32
- value_rows: bfloat16 [32768, 1024], P('ctx', 'head'), may hold values from -6 to 6
- out_weight: bfloat16 [4096, 4096], P('head', 'ctx'), may hold values from -0.71875 to 0.71875
Outputs:
- attended: bfloat16 [32768, 4096], P('ctx', 'head')
All inputs are finite; a program needn't handle non-finite values.
Results may differ from a plain program's by a relative error of at most 0.015.
Values may be sent and summed in bfloat16 or wider, within the bound.
A program may use at most 64 MiB of HBM per device.

v0:
```python
import jax
import jax.numpy as jnp
from jax import lax
from jax.sharding import PartitionSpec as P

HD = 128
BLOCK = 512


def from_partner(shard, axis, bit):
    return lax.ppermute(shard, axis, [(i, i ^ 1 << bit) for i in range(lax.axis_size(axis))])


def combine(state, update):
    peak_old, total_old, output_old = state
    peak_new, total_new, output_new = update
    top = jnp.maximum(peak_old, peak_new)
    scale_old = jnp.exp(peak_old - top)
    scale_new = jnp.exp(peak_new - top)
    total = scale_old * total_old + scale_new * total_new
    output = scale_old[..., None] * output_old + scale_new[..., None] * output_new
    return (top, total, output)


def shards(query_rows, key_rows, value_rows, out_weight):
    tok_rows, query_cols = query_rows.shape
    block_count = tok_rows // BLOCK
    heads_kv = key_rows.shape[1] // HD
    heads_query = query_cols // HD
    group = heads_query // heads_kv
    queries = query_rows.reshape(block_count, BLOCK, heads_kv, group, HD)
    stacked = jnp.stack(
        [
            key_rows.reshape(block_count, BLOCK, heads_kv, HD),
            value_rows.reshape(block_count, BLOCK, heads_kv, HD),
        ]
    )
    factor = HD ** (-0.5)

    def block_stats(pair):
        scores = (
            jnp.einsum("bqgrd,bkgd->bgrqk", queries, pair[0], preferred_element_type=jnp.float32)
            * factor
        )
        peak = jnp.max(scores, axis=-1)
        weights = jnp.exp(scores - peak[..., None])
        total = jnp.sum(weights, axis=-1)
        probs = weights.astype(jnp.bfloat16)
        output = jnp.einsum("bgrqk,bkgd->bgrqd", probs, pair[1], preferred_element_type=jnp.float32)
        return (peak, total, output)

    state = block_stats(stacked)
    level_list = list(range(lax.axis_size("ctx").bit_length() - 1))
    for level in level_list:
        partner = from_partner(stacked, "ctx", level)
        state = combine(state, block_stats(partner))
    hidden = state[2] / state[1][..., None]
    hidden = hidden.transpose(0, 3, 1, 2, 4).reshape(tok_rows, query_cols).astype(jnp.bfloat16)
    terms = jnp.dot(
        hidden,
        lax.all_gather(out_weight, "ctx", axis=1, tiled=True),
        preferred_element_type=jnp.float32,
    )
    return lax.psum_scatter(terms.astype(jnp.bfloat16), "head", scatter_dimension=1, tiled=True)


def solution(mesh):
    placed = (P("ctx", "head"), P("ctx", "head"), P("ctx", "head"), P("head", "ctx"))
    return jax.shard_map(
        shards, mesh=mesh, in_specs=placed, out_specs=P("ctx", "head"), check_vma=False
    )
```

profile of v0, /device:TPU:1, one launch (start us, length us, event | category | flops | bytes accessed | tf_op | source)
XLA Modules:
  0.0 273.2 jit_solution(7072032613657819309)
XLA Ops:
  6.5 0.7 all-gather.2.cloned.1.call-update
  7.3 1.0 pad_maximum_fusion
  8.3 3.9 %collective-permute-start.3 = (bf16[2,1,512,1,128]{4,2,3,1,0:T(8,128)(2,1)S(1)}, bf16[2,1,512,1,128]{4,2,3,1,0:T(8,128)(2,1)S(1)}, u32[]{:S(2)}, u32[]{:S(2)}) collective-permute-start(bf16[2,1,512,1,128]{4,2,3,1,0:T(8,128)(2,1)S(1)} %pad_maximum_fusion), channel_id=1, source_target_pairs={{0,64},{8,72},{16,80},{24,88},{32,96},{40,104},{48,112},{56,120},{... | collective-permute-start | bytes 786440 | tf_op jit(solution)/shard_map/ppermute | solution.py:11
  12.3 4.8 %collective-permute-start.2 = (bf16[2,1,512,1,128]{4,2,3,1,0:T(8,128)(2,1)S(1)}, bf16[2,1,512,1,128]{4,2,3,1,0:T(8,128)(2,1)S(1)}, u32[]{:S(2)}, u32[]{:S(2)}) collective-permute-start(bf16[2,1,512,1,128]{4,2,3,1,0:T(8,128)(2,1)S(1)} %pad_maximum_fusion), channel_id=1, source_target_pairs={{0,32},{8,40},{16,48},{24,56},{32,0},{40,8},{48,16},{56,24},{64,96... | collective-permute-start | bytes 786440 | tf_op jit(solution)/shard_map/ppermute | solution.py:11
  17.1 2.3 collective-permute-start.1
  19.4 3.5 %collective-permute-start = (bf16[2,1,512,1,128]{4,2,3,1,0:T(8,128)(2,1)S(1)}, bf16[2,1,512,1,128]{4,2,3,1,0:T(8,128)(2,1)S(1)}, u32[]{:S(2)}, u32[]{:S(2)}) collective-permute-start(bf16[2,1,512,1,128]{4,2,3,1,0:T(8,128)(2,1)S(1)} %pad_maximum_fusion), channel_id=1, source_target_pairs={{0,8},{8,0},{16,24},{24,16},{32,40},{40,32},{48,56},{56,48},{64,72... | collective-permute-start | bytes 786440 | tf_op jit(solution)/shard_map/ppermute | solution.py:11
  22.9 4.3 %collective-permute-start.4 = (bf16[2,1,512,1,128]{4,2,3,1,0:T(8,128)(2,1)S(1)}, bf16[2,1,512,1,128]{4,2,3,1,0:T(8,128)(2,1)S(1)}, u32[]{:S(2)}, u32[]{:S(2)}) collective-permute-start(bf16[2,1,512,1,128]{4,2,3,1,0:T(8,128)(2,1)S(1)} %pad_maximum_fusion), channel_id=1, source_target_pairs={{0,128},{8,136},{16,144},{24,152},{32,160},{40,168},{48,176},{56,1... | collective-permute-start | bytes 786440 | tf_op jit(solution)/shard_map/ppermute | solution.py:11
  27.2 1.6 bitcast_reduce_fusion.6
  28.8 0.7 fusion.7
  29.6 15.4 %collective-permute-start.5 = (bf16[2,1,512,1,128]{4,2,3,1,0:T(8,128)(2,1)S(1)}, bf16[2,1,512,1,128]{4,2,3,1,0:T(8,128)(2,1)S(1)}, u32[]{:S(2)}, u32[]{:S(2)}) collective-permute-start(bf16[2,1,512,1,128]{4,2,3,1,0:T(8,128)(2,1)S(1)} %pad_maximum_fusion), channel_id=1, source_target_pairs={{0,256},{8,264},{16,272},{24,280},{32,288},{40,296},{48,304},{56,3... | collective-permute-start | bytes 786440 | tf_op jit(solution)/shard_map/ppermute | solution.py:11
  45.0 0.7 bitcast_reduce_fusion.4
  45.7 0.7 fusion.11
  46.5 0.7 bitcast_reduce_fusion.3
  47.2 0.7 fusion.13
  47.9 0.7 bitcast_reduce_fusion.2
  48.6 0.7 fusion.15
  49.3 0.7 bitcast_reduce_fusion.5
  50.1 0.7 fusion.9
  50.8 0.7 bitcast_reduce_fusion.1
  51.5 0.7 fusion.17
  52.2 4.7 %collective-permute-done.5 = bf16[2,1,512,1,128]{4,2,3,1,0:T(8,128)(2,1)S(1)} collective-permute-done((bf16[2,1,512,1,128]{4,2,3,1,0:T(8,128)(2,1)S(1)}, bf16[2,1,512,1,128]{4,2,3,1,0:T(8,128)(2,1)S(1)}, u32[]{:S(2)}, u32[]{:S(2)}) %collective-permute-start.5) | collective-permute-done | bytes 262176 | tf_op jit(solution)/shard_map/ppermute | solution.py:11
  56.9 0.7 bitcast_reduce_fusion
  58.5 0.9 fusion.56
  59.4 0.9 fusion.77
  60.3 0.9 fusion.80
  61.3 0.9 fusion.83
  62.2 1.1 fusion.86
  63.3 0.9 fusion.89
  64.3 1.7 fusion.113
  66.0 99.9 %all-gather.2.cloned.1.call-done = bf16[512,4096]{0,1:T(8,128)(2,1)} async-done(((bf16[512,64]{0,1:T(8,128)(2,1)}), bf16[512,4096]{0,1:T(8,128)(2,1)}) %all-gather.2.cloned.1.call-update) | async-done | bytes 4194320 | tf_op jit(solution)/shard_map/all_gather | solution.py:61
  165.8 6.6 %convolution_convert_fusion = bf16[512,4096]{1,0:T(8,128)(2,1)} fusion(bf16[512,512]{0,1:T(8,128)(2,1)S(1)} %bitcast.339, bf16[512,4096]{0,1:T(8,128)(2,1)} %all-gather.2.cloned.1.call-done), kind=kOutput, calls=%fused_computation | convolution fusion | flops 2149580800 | bytes 8912896 | tf_op jit(solution)/shard_map/dot_general | solution.py:59
  172.4 94.0 %reduce-scatter.2.cloned.1.call-done = bf16[512,512]{1,0:T(8,128)(2,1)} async-done(((bf16[512,4096]{1,0:T(8,128)(2,1)}), bf16[512,512]{1,0:T(8,128)(2,1)}) %reduce-scatter.2.cloned.1.call-update) | async-done | bytes 524304 | tf_op jit(solution)/shard_map/reduce_scatter | solution.py:64
  (15 shorter events, 0.9 us)
Async XLA Ops:
  6.5 20.7 %copy-start = (bf16[512,512]{1,0:T(8,128)(2,1)S(1)}, bf16[512,512]{1,0:T(8,128)(2,1)}, u32[]{:S(2)}) copy-start(bf16[512,512]{1,0:T(8,128)(2,1)} %param.4) | copy-start | bytes 1572868
  6.5 159.3 %all-gather.2.cloned.1.call-start = ((), (), s32[]{:S(2)}) async-start(), calls=%async_computation.1 | async-start | bytes 4259840 | tf_op jit(solution)/shard_map/all_gather | solution.py:61
  7.3 259.1 %reduce-scatter.2.cloned.1.call-start = ((), (), s32[]{:S(2)}) async-start(), calls=%async_computation.2 | async-start | bytes 4718592 | tf_op jit(solution)/shard_map/reduce_scatter | solution.py:64
  8.3 39.6 %collective-permute-start.3 = (bf16[2,1,512,1,128]{4,2,3,1,0:T(8,128)(2,1)S(1)}, bf16[2,1,512,1,128]{4,2,3,1,0:T(8,128)(2,1)S(1)}, u32[]{:S(2)}, u32[]{:S(2)}) collective-permute-start(bf16[2,1,512,1,128]{4,2,3,1,0:T(8,128)(2,1)S(1)} %pad_maximum_fusion), channel_id=1, source_target_pairs={{0,64},{8,72},{16,80},{24,88},{32,96},{40,104},{48,112},{56,120},{... | collective-permute-start | bytes 786440 | tf_op jit(solution)/shard_map/ppermute | solution.py:11
  12.3 34.2 %collective-permute-start.2 = (bf16[2,1,512,1,128]{4,2,3,1,0:T(8,128)(2,1)S(1)}, bf16[2,1,512,1,128]{4,2,3,1,0:T(8,128)(2,1)S(1)}, u32[]{:S(2)}, u32[]{:S(2)}) collective-permute-start(bf16[2,1,512,1,128]{4,2,3,1,0:T(8,128)(2,1)S(1)} %pad_maximum_fusion), channel_id=1, source_target_pairs={{0,32},{8,40},{16,48},{24,56},{32,0},{40,8},{48,16},{56,24},{64,96... | collective-permute-start | bytes 786440 | tf_op jit(solution)/shard_map/ppermute | solution.py:11
  17.1 12.5 %collective-permute-start.1 = (bf16[2,1,512,1,128]{4,2,3,1,0:T(8,128)(2,1)S(1)}, bf16[2,1,512,1,128]{4,2,3,1,0:T(8,128)(2,1)S(1)}, u32[]{:S(2)}, u32[]{:S(2)}) collective-permute-start(bf16[2,1,512,1,128]{4,2,3,1,0:T(8,128)(2,1)S(1)} %pad_maximum_fusion), channel_id=1, source_target_pairs={{0,16},{8,24},{16,0},{24,8},{32,48},{40,56},{48,32},{56,40},{64,80... | collective-permute-start | bytes 786440 | tf_op jit(solution)/shard_map/ppermute | solution.py:11
  19.4 29.9 %collective-permute-start = (bf16[2,1,512,1,128]{4,2,3,1,0:T(8,128)(2,1)S(1)}, bf16[2,1,512,1,128]{4,2,3,1,0:T(8,128)(2,1)S(1)}, u32[]{:S(2)}, u32[]{:S(2)}) collective-permute-start(bf16[2,1,512,1,128]{4,2,3,1,0:T(8,128)(2,1)S(1)} %pad_maximum_fusion), channel_id=1, source_target_pairs={{0,8},{8,0},{16,24},{24,16},{32,40},{40,32},{48,56},{56,48},{64,72... | collective-permute-start | bytes 786440 | tf_op jit(solution)/shard_map/ppermute | solution.py:11
  22.9 27.9 %collective-permute-start.4 = (bf16[2,1,512,1,128]{4,2,3,1,0:T(8,128)(2,1)S(1)}, bf16[2,1,512,1,128]{4,2,3,1,0:T(8,128)(2,1)S(1)}, u32[]{:S(2)}, u32[]{:S(2)}) collective-permute-start(bf16[2,1,512,1,128]{4,2,3,1,0:T(8,128)(2,1)S(1)} %pad_maximum_fusion), channel_id=1, source_target_pairs={{0,128},{8,136},{16,144},{24,152},{32,160},{40,168},{48,176},{56,1... | collective-permute-start | bytes 786440 | tf_op jit(solution)/shard_map/ppermute | solution.py:11
  29.6 27.4 %collective-permute-start.5 = (bf16[2,1,512,1,128]{4,2,3,1,0:T(8,128)(2,1)S(1)}, bf16[2,1,512,1,128]{4,2,3,1,0:T(8,128)(2,1)S(1)}, u32[]{:S(2)}, u32[]{:S(2)}) collective-permute-start(bf16[2,1,512,1,128]{4,2,3,1,0:T(8,128)(2,1)S(1)} %pad_maximum_fusion), channel_id=1, source_target_pairs={{0,256},{8,264},{16,272},{24,280},{32,288},{40,296},{48,304},{56,3... | collective-permute-start | bytes 786440 | tf_op jit(solution)/shard_map/ppermute | solution.py:11
  52.2 6.2 %copy-start.1 = (bf16[512,128]{1,0:T(8,128)(2,1)S(1)}, bf16[512,128]{1,0:T(8,128)(2,1)}, u32[]{:S(2)}) copy-start(bf16[512,128]{1,0:T(8,128)(2,1)} %param.6) | copy-start | bytes 393220
Sparse Core Ops, SparseCore 0:
  11.9 153.8 all-gather.1
  172.5 93.8 reduce-scatter.1
where the time goes:
time: 274 us; the launch traced here: 273 us
  waiting for transfers between devices  199 us (73%)
  starting transfers between devices  34.3 us (13%)
  matrix products  20 us (7%)
  between operations  13.6 us (5%)
  other arithmetic  6 us (2%)
    all_gather x1, waiting for transfers between devices, shards(): lax.all_gather(out_weight, 'ctx', axis=1, tiled=True)  99.9 us
    reduce_scatter x1, waiting for transfers between devices, shards(): lax.psum_scatter(terms.astype(jnp.bfloat16), 'head', scatter_dimension=1,...  94 us
    ppermute x6, starting transfers between devices, from_partner(): lax.ppermute(shard, axis, [(i, i ^ 1 << bit) for i in range(lax.axis_size...  34.3 us
    dot_general x7, matrix products, block_stats(): jnp.einsum('bgrqk,bkgd->bgrqd', probs, pair[1], preferred_element_type=jn...  7.46 us
    dot_general x1, matrix products, shards(): jnp.dot(hidden, lax.all_gather(out_weight, 'ctx', axis=1, tiled=True), pr...  6.56 us
    dot_general x7, matrix products, block_stats(): jnp.einsum('bqgrd,bkgd->bgrqk', queries, pair[0], preferred_element_type=...  5.96 us
  transfers between devices with their start and end apart: 8, of which 3 were waited for; matrix products, arithmetic and copies ran while one was open for 7% of the time, Pallas kernels for 0%

commit v1 on v0

--- a/solution.py
+++ b/solution.py
@@ -5,6 +5,13 @@
 
 HD = 128
 BLOCK = 512
+
+
+def all_by_exchange(array, name, d):
+    peers = lax.axis_size(name)
+    blocks = jnp.stack([array for _ in range(peers)])
+    blocks = lax.all_to_all(blocks, name, split_axis=0, concat_axis=0)
+    return jnp.concatenate(blocks, axis=d)
 
 
 def from_partner(shard, axis, bit):
@@ -57,9 +64,7 @@
     hidden = state[2] / state[1][..., None]
     hidden = hidden.transpose(0, 3, 1, 2, 4).reshape(tok_rows, query_cols).astype(jnp.bfloat16)
     terms = jnp.dot(
-        hidden,
-        lax.all_gather(out_weight, "ctx", axis=1, tiled=True),
-        preferred_element_type=jnp.float32,
+        hidden, all_by_exchange(out_weight, "ctx", 1), preferred_element_type=jnp.float32
     )
     return lax.psum_scatter(terms.astype(jnp.bfloat16), "head", scatter_dimension=1, tiled=True)
 

time: 274 us -> 368 us (1.34)
  waiting for transfers between devices: 199 us -> 270 us
  starting transfers between devices: 34.3 us -> 55.4 us
    reduce_scatter x1, waiting for transfers between devices: 94 us -> 196 us  [shards(): lax.psum_scatter(terms.astype(jnp.bfloat16), 'head', scatter_dimension=1,...]
    all_gather x1 -> x0, waiting for transfers between devices: 99.9 us -> none  [shards(): lax.all_gather(out_weight, 'ctx', axis=1, tiled=True)]
    ppermute x6, waiting for transfers between devices: 4.72 us -> 74.6 us  [from_partner(): lax.ppermute(shard, axis, [(i, i ^ 1 << bit) for i in range(lax.axis_size...]
    all_to_all x0 -> x1, starting transfers between devices: none -> 22.6 us  [all_by_exchange(): blocks = lax.all_to_all(blocks, name, split_axis=0, concat_axis=0)]
  transfers between devices with their start and end apart: 8 -> 8, of which waited for: 3 -> 3; matrix products, arithmetic and copies ran while one was open for 7% -> 5% of each run, Pallas kernels for 0% -> 0%
where the time goes in v1:
time: 368 us; the launch traced here: 367 us
  waiting for transfers between devices  270 us (73%)
  starting transfers between devices  55.4 us (15%)
  matrix products  19.2 us (5%)
  between operations  13.6 us (4%)
  other arithmetic  5.04 us (1%)
    reduce_scatter x1, waiting for transfers between devices, shards(): lax.psum_scatter(terms.astype(jnp.bfloat16), 'head', scatter_dimension=1,...  196 us
    ppermute x6, waiting for transfers between devices, from_partner(): lax.ppermute(shard, axis, [(i, i ^ 1 << bit) for i in range(lax.axis_size...  74.6 us
    ppermute x6, starting transfers between devices, from_partner(): lax.ppermute(shard, axis, [(i, i ^ 1 << bit) for i in range(lax.axis_size...  32.8 us
    all_to_all x1, starting transfers between devices, all_by_exchange(): blocks = lax.all_to_all(blocks, name, split_axis=0, concat_axis=0)  22.6 us
    dot_general x7, matrix products, block_stats(): jnp.einsum('bgrqk,bkgd->bgrqd', probs, pair[1], preferred_element_type=jn...  7.51 us
  transfers between devices with their start and end apart: 8, of which 3 were waited for; matrix products, arithmetic and copies ran while one was open for 5% of the time, Pallas kernels for 0%

profile of v1, /device:TPU:1, one launch (start us, length us, event | category | flops | bytes accessed | tf_op | source)
XLA Modules:
  0.0 367.1 jit_solution(3094345737703187149)
XLA Ops:
  6.5 3.4 stack.5
  9.9 22.6 %all-to-all-start = ((bf16[64,512,64]{1,2,0:T(8,128)(2,1)}), bf16[64,512,64]{1,2,0:T(8,128)(2,1)}, u32[]{:S(2)}, u32[]{:S(2)}) async-start(bf16[64,512,64]{1,2,0:T(8,128)(2,1)} %stack.5), calls=%async_computation | async-start | bytes 8388608 | tf_op jit(solution)/shard_map/all_to_all | solution.py:13
  32.6 3.3 collective-permute-start.3
  35.9 4.6 %collective-permute-start.2 = (bf16[2,1,512,1,128]{4,2,3,1,0:T(8,128)(2,1)S(1)}, bf16[2,1,512,1,128]{4,2,3,1,0:T(8,128)(2,1)S(1)}, u32[]{:S(2)}, u32[]{:S(2)}) collective-permute-start(bf16[2,1,512,1,128]{4,2,3,1,0:T(8,128)(2,1)S(1)} %pad_maximum_fusion), channel_id=1, source_target_pairs={{0,32},{8,40},{16,48},{24,56},{32,0},{40,8},{48,16},{56,24},{64,96... | collective-permute-start | bytes 786440 | tf_op jit(solution)/shard_map/ppermute | solution.py:18
  40.5 2.2 collective-permute-start.1
  42.7 3.1 collective-permute-start
  45.8 4.4 %collective-permute-start.4 = (bf16[2,1,512,1,128]{4,2,3,1,0:T(8,128)(2,1)S(1)}, bf16[2,1,512,1,128]{4,2,3,1,0:T(8,128)(2,1)S(1)}, u32[]{:S(2)}, u32[]{:S(2)}) collective-permute-start(bf16[2,1,512,1,128]{4,2,3,1,0:T(8,128)(2,1)S(1)} %pad_maximum_fusion), channel_id=1, source_target_pairs={{0,128},{8,136},{16,144},{24,152},{32,160},{40,168},{48,176},{56,1... | collective-permute-start | bytes 786440 | tf_op jit(solution)/shard_map/ppermute | solution.py:18
  50.2 0.7 bitcast_reduce_fusion.6
  50.9 0.7 fusion.7
  51.6 31.9 %collective-permute-done.1 = bf16[2,1,512,1,128]{4,2,3,1,0:T(8,128)(2,1)S(1)} collective-permute-done((bf16[2,1,512,1,128]{4,2,3,1,0:T(8,128)(2,1)S(1)}, bf16[2,1,512,1,128]{4,2,3,1,0:T(8,128)(2,1)S(1)}, u32[]{:S(2)}, u32[]{:S(2)}) %collective-permute-start.1) | collective-permute-done | bytes 262176 | tf_op jit(solution)/shard_map/ppermute | solution.py:18
  83.6 15.3 %collective-permute-start.5 = (bf16[2,1,512,1,128]{4,2,3,1,0:T(8,128)(2,1)S(1)}, bf16[2,1,512,1,128]{4,2,3,1,0:T(8,128)(2,1)S(1)}, u32[]{:S(2)}, u32[]{:S(2)}) collective-permute-start(bf16[2,1,512,1,128]{4,2,3,1,0:T(8,128)(2,1)S(1)} %pad_maximum_fusion), channel_id=1, source_target_pairs={{0,256},{8,264},{16,272},{24,280},{32,288},{40,296},{48,304},{56,3... | collective-permute-start | bytes 786440 | tf_op jit(solution)/shard_map/ppermute | solution.py:18
  98.8 0.7 bitcast_reduce_fusion.4
  99.6 0.7 fusion.11
  100.3 0.7 bitcast_reduce_fusion.3
  101.0 0.7 fusion.13
  101.7 0.7 bitcast_reduce_fusion.2
  102.5 0.7 fusion.15
  103.2 0.7 bitcast_reduce_fusion.5
  103.9 0.7 fusion.9
  104.6 0.7 bitcast_reduce_fusion.1
  105.4 0.7 fusion.17
  106.1 42.7 %collective-permute-done.5 = bf16[2,1,512,1,128]{4,2,3,1,0:T(8,128)(2,1)S(1)} collective-permute-done((bf16[2,1,512,1,128]{4,2,3,1,0:T(8,128)(2,1)S(1)}, bf16[2,1,512,1,128]{4,2,3,1,0:T(8,128)(2,1)S(1)}, u32[]{:S(2)}, u32[]{:S(2)}) %collective-permute-start.5) | collective-permute-done | bytes 262176 | tf_op jit(solution)/shard_map/ppermute | solution.py:18
  148.8 0.7 bitcast_reduce_fusion
  150.3 0.9 fusion.56
  151.2 0.9 fusion.77
  152.2 0.9 fusion.80
  153.1 0.9 fusion.83
  154.1 1.2 fusion.86
  155.2 0.9 fusion.89
  156.2 1.7 fusion.113
  157.9 6.6 %convolution_convert_fusion = bf16[512,4096]{1,0:T(8,128)(2,1)} fusion(bf16[512,512]{0,1:T(8,128)(2,1)S(1)} %bitcast.342, bf16[512,4096]{0,1:T(8,128)(2,1)} %bitcast.60), kind=kOutput, calls=%fused_computation | convolution fusion | flops 2149580800 | bytes 8912896 | tf_op jit(solution)/shard_map/dot_general | solution.py:66
  164.5 195.8 %reduce-scatter.2.cloned.1.call-done = bf16[512,512]{1,0:T(8,128)(2,1)} async-done(((bf16[512,4096]{1,0:T(8,128)(2,1)}), bf16[512,512]{1,0:T(8,128)(2,1)}) %reduce-scatter.2.cloned.1.call-update) | async-done | bytes 524304 | tf_op jit(solution)/shard_map/reduce_scatter | solution.py:69
  (17 shorter events, 0.9 us)
Async XLA Ops:
  6.5 43.7 %copy-start = (bf16[512,512]{1,0:T(8,128)(2,1)S(1)}, bf16[512,512]{1,0:T(8,128)(2,1)}, u32[]{:S(2)}) copy-start(bf16[512,512]{1,0:T(8,128)(2,1)} %param.4) | copy-start | bytes 1572868
  9.9 22.6 %copy-start.1 = (bf16[512,128]{1,0:T(8,128)(2,1)S(1)}, bf16[512,128]{1,0:T(8,128)(2,1)}, u32[]{:S(2)}) copy-start(bf16[512,128]{1,0:T(8,128)(2,1)} %param.5) | copy-start | bytes 393220
  9.9 22.6 %copy-start.2 = (bf16[512,128]{1,0:T(8,128)(2,1)S(1)}, bf16[512,128]{1,0:T(8,128)(2,1)}, u32[]{:S(2)}) copy-start(bf16[512,128]{1,0:T(8,128)(2,1)} %param.6) | copy-start | bytes 393220
  9.9 147.9 %all-to-all-start = ((bf16[64,512,64]{1,2,0:T(8,128)(2,1)}), bf16[64,512,64]{1,2,0:T(8,128)(2,1)}, u32[]{:S(2)}, u32[]{:S(2)}) async-start(bf16[64,512,64]{1,2,0:T(8,128)(2,1)} %stack.5), calls=%async_computation | async-start | bytes 8388608 | tf_op jit(solution)/shard_map/all_to_all | solution.py:13
  32.5 327.8 %reduce-scatter.2.cloned.1.call-start = ((), (), s32[]{:S(2)}) async-start(), calls=%async_computation.2 | async-start | bytes 4718592 | tf_op jit(solution)/shard_map/reduce_scatter | solution.py:69
  32.6 69.1 %collective-permute-start.3 = (bf16[2,1,512,1,128]{4,2,3,1,0:T(8,128)(2,1)S(1)}, bf16[2,1,512,1,128]{4,2,3,1,0:T(8,128)(2,1)S(1)}, u32[]{:S(2)}, u32[]{:S(2)}) collective-permute-start(bf16[2,1,512,1,128]{4,2,3,1,0:T(8,128)(2,1)S(1)} %pad_maximum_fusion), channel_id=1, source_target_pairs={{0,64},{8,72},{16,80},{24,88},{32,96},{40,104},{48,112},{56,120},{... | collective-permute-start | bytes 786440 | tf_op jit(solution)/shard_map/ppermute | solution.py:18
  35.9 64.4 %collective-permute-start.2 = (bf16[2,1,512,1,128]{4,2,3,1,0:T(8,128)(2,1)S(1)}, bf16[2,1,512,1,128]{4,2,3,1,0:T(8,128)(2,1)S(1)}, u32[]{:S(2)}, u32[]{:S(2)}) collective-permute-start(bf16[2,1,512,1,128]{4,2,3,1,0:T(8,128)(2,1)S(1)} %pad_maximum_fusion), channel_id=1, source_target_pairs={{0,32},{8,40},{16,48},{24,56},{32,0},{40,8},{48,16},{56,24},{64,96... | collective-permute-start | bytes 786440 | tf_op jit(solution)/shard_map/ppermute | solution.py:18
  40.5 43.1 %collective-permute-start.1 = (bf16[2,1,512,1,128]{4,2,3,1,0:T(8,128)(2,1)S(1)}, bf16[2,1,512,1,128]{4,2,3,1,0:T(8,128)(2,1)S(1)}, u32[]{:S(2)}, u32[]{:S(2)}) collective-permute-start(bf16[2,1,512,1,128]{4,2,3,1,0:T(8,128)(2,1)S(1)} %pad_maximum_fusion), channel_id=1, source_target_pairs={{0,16},{8,24},{16,0},{24,8},{32,48},{40,56},{48,32},{56,40},{64,80... | collective-permute-start | bytes 786440 | tf_op jit(solution)/shard_map/ppermute | solution.py:18
  42.7 60.5 %collective-permute-start = (bf16[2,1,512,1,128]{4,2,3,1,0:T(8,128)(2,1)S(1)}, bf16[2,1,512,1,128]{4,2,3,1,0:T(8,128)(2,1)S(1)}, u32[]{:S(2)}, u32[]{:S(2)}) collective-permute-start(bf16[2,1,512,1,128]{4,2,3,1,0:T(8,128)(2,1)S(1)} %pad_maximum_fusion), channel_id=1, source_target_pairs={{0,8},{8,0},{16,24},{24,16},{32,40},{40,32},{48,56},{56,48},{64,72... | collective-permute-start | bytes 786440 | tf_op jit(solution)/shard_map/ppermute | solution.py:18
  45.8 58.8 %collective-permute-start.4 = (bf16[2,1,512,1,128]{4,2,3,1,0:T(8,128)(2,1)S(1)}, bf16[2,1,512,1,128]{4,2,3,1,0:T(8,128)(2,1)S(1)}, u32[]{:S(2)}, u32[]{:S(2)}) collective-permute-start(bf16[2,1,512,1,128]{4,2,3,1,0:T(8,128)(2,1)S(1)} %pad_maximum_fusion), channel_id=1, source_target_pairs={{0,128},{8,136},{16,144},{24,152},{32,160},{40,168},{48,176},{56,1... | collective-permute-start | bytes 786440 | tf_op jit(solution)/shard_map/ppermute | solution.py:18
  83.6 65.2 %collective-permute-start.5 = (bf16[2,1,512,1,128]{4,2,3,1,0:T(8,128)(2,1)S(1)}, bf16[2,1,512,1,128]{4,2,3,1,0:T(8,128)(2,1)S(1)}, u32[]{:S(2)}, u32[]{:S(2)}) collective-permute-start(bf16[2,1,512,1,128]{4,2,3,1,0:T(8,128)(2,1)S(1)} %pad_maximum_fusion), channel_id=1, source_target_pairs={{0,256},{8,264},{16,272},{24,280},{32,288},{40,296},{48,304},{56,3... | collective-permute-start | bytes 786440 | tf_op jit(solution)/shard_map/ppermute | solution.py:18
Sparse Core Ops, SparseCore 0:
  164.6 195.6 reduce-scatter.1
